TPU v7x, 32 devices: a whole 2x2x4 slice. The times are simulated.
32 devices in a mesh: energy: 8 (over y, x, core), space: 4 (over z).
Axes of the slice: x: 2, y: 2, z: 4, core: 2. Of those that a mesh axis runs over, the one named last changes fastest.
Arguments:
- onsite: float32 [4, 2, 128, 128], P('space'), may hold values from -0.25 to 0.25
- hopping: float32 [4, 2, 128, 128], P('space'), may hold values from -0.25 to 0.25
- sigma_old: float32 [8, 4, 2, 128, 128], P('energy', 'space'), may hold values from -0.0390625 to 0.0390625
- screened: float32 [8, 4, 2, 3, 2, 128, 128], P('energy', 'space'), may hold values from -2 to 2
Outputs:
- green_retarded: float32 [8, 4, 3, 2, 128, 128], P('energy', 'space')
- self_energy: float32 [8, 4, 2, 3, 2, 128, 128], P('energy', 'space')
All inputs are finite; a program needn't handle non-finite values.
Results may differ from a plain program's by a relative error of at most 0.0003.
Values sent between devices are 32-bit elements; how exact they have to be, the bound alone decides.
No kernel may reach another device: no remote copies, remote signals or barrier semaphores. Data moves between devices by JAX's collectives and lax.ppermute only.
A program may use at most 128 MiB of HBM per device.

v0:
```python
import functools
import math

import jax
import jax.numpy as jnp
from jax import lax
from jax.experimental import pallas as pl
from jax.experimental.pallas import tpu as pltpu
from jax.sharding import PartitionSpec as P

BROADEN = 0.45
THERMAL = 0.1
F32 = jnp.float32
BF16 = jnp.bfloat16

LOWEST = 1.0 / 128.0
SQUARINGS = 6
DONE = 1e-4
STEPS_MAX = 60
WORK = 1
WORK2 = 8
WORK3 = 1
WORK4 = 1
WORK5 = 0.01
WORK6 = 1


def schedule():
    rho = (1.0 - LOWEST) / (1.0 + LOWEST)
    scales = []
    for _ in range(SQUARINGS):
        scales.append(2.0 / (2.0 - rho * rho))
        rho = rho * rho / (2.0 - rho * rho)
    return 2.0 / (1.0 + LOWEST), scales


def real_of(x):
    return x[:, : x.shape[1] // 2]


def imag_of(x):
    return x[:, x.shape[1] // 2 :]


def wide(x):
    return jnp.concatenate([x, jnp.concatenate([-imag_of(x), real_of(x)], axis=1)], axis=0)


def dagger(x):
    return jnp.concatenate([real_of(x).T, -imag_of(x).T], axis=1)


def dot(a, b):
    return jnp.dot(a, b, preferred_element_type=F32)


def split(x):
    high = x.astype(BF16)
    return high, (x - high.astype(F32)).astype(BF16)


def product(a, b):
    rows = a.shape[0]
    a_high, a_low = split(a)
    b_high, b_low = split(b)
    both = dot(jnp.concatenate([a_high, a_low], axis=0), wide(b_high))
    return both[:rows] + both[rows:] + dot(a_high, wide(b_low))


def times_complex(x, re, im):
    return jnp.concatenate(
        [re * real_of(x) - im * imag_of(x), re * imag_of(x) + im * real_of(x)], axis=1
    )


def identity_like(x):
    size = x.shape[0]
    row = lax.broadcasted_iota(jnp.int32, x.shape, 0)
    column = lax.broadcasted_iota(jnp.int32, x.shape, 1)
    return jnp.where(row == column, 1.0, 0.0).astype(F32)


def largest(x, axis):
    return jnp.max(x, axis=axis, keepdims=True)


def invert(s, out_ref):
    size = s.shape[0]
    one = identity_like(s)
    first, scales = schedule()
    s_dagger = dagger(s)
    s_dagger_b = s_dagger.astype(BF16)
    normal = dot(s.astype(BF16), wide(s_dagger_b))
    normal_b = normal.astype(BF16)
    both = dot(jnp.concatenate([s_dagger_b, normal_b], axis=0), wide(normal_b))
    square = both[size:]
    sums = jnp.sum(jnp.sqrt(real_of(square) ** 2 + imag_of(square) ** 2), axis=0, keepdims=True)
    a = first * lax.rsqrt(largest(sums, 1))
    c = scales[0]
    x = (2.0 * c * a) * s_dagger - (c * a * a) * both[:size]
    r = one - (2.0 * c * a) * normal + (c * a * a) * square
    for c in scales[1:]:
        r_b = r.astype(BF16)
        both = dot(jnp.concatenate([x.astype(BF16), r_b], axis=0), wide(r_b))
        x = c * (x + both[:size])
        r = (1.0 - c) * one + c * both[size:]
    s_high, s_low = split(s)
    s_both = jnp.concatenate([s_high, s_low], axis=0)
    x_b = x.astype(BF16)
    both = dot(s_both, wide(x_b))
    e_b = (one - both[:size] - both[size:]).astype(BF16)
    x = x_b.astype(F32) + dot(x_b, wide(e_b))

    def step(x):
        x_high, x_low = split(x)
        both = dot(s_both, wide(x_high))
        e = one - both[:size] - both[size:] - dot(s_high, wide(x_low))
        return x + dot(x_high, wide(e.astype(BF16))), jnp.sum(e * e)

    x, left = step(x)
    out_ref[...] = x

    @pl.when(jnp.logical_not(left < DONE))
    def _():
        bound = jnp.sqrt(largest(jnp.sum(jnp.abs(s), axis=1, keepdims=True), 0))
        other = jnp.sqrt(largest(jnp.sum(jnp.abs(real_of(s)) + jnp.abs(imag_of(s)), axis=0, keepdims=True), 1))
        safe = s_dagger / (bound * bound) / (other * other)
        good = left < 0.5
        start = jnp.where(good, x, safe)

        def unfinished(state):
            count, value, _ = state
            return jnp.logical_and(count < STEPS_MAX, jnp.logical_not(value < DONE))

        def body(state):
            count, _, x = state
            new = product(x, one - product(s, x))
            e = one - product(s, x)
            return count + 1, jnp.sum(e * e), x + new

        _, _, result = lax.while_loop(unfinished, body, (0, left, start))
        out_ref[...] = result


def energy_at(index, energies_all):
    return -1.5 + 3.0 * (index + 0.5) / energies_all


def energy_point(axes):
    chips, cores, _ = axes
    index = lax.axis_index("chip") * cores + lax.axis_index("core")
    return energy_at(index.astype(F32), chips * cores)


def place(axes):
    position, cells_all = lax.axis_index("space"), axes[2]
    return position, jnp.minimum(position, cells_all - 1 - position), position < cells_all // 2


def outer_kernel(
    axes, onsite_far, hopping_far, sigma_far, system_ref, green_ref, message_ref, h_ref, hd_ref, token_ref, onsite, hopping, sigma, arrivals
):
    copies = [
        pltpu.make_async_copy(far, near, arrivals.at[i])
        for i, (far, near) in enumerate(((onsite_far, onsite), (hopping_far, hopping), (sigma_far, sigma)))
    ]
    for copy in copies:
        copy.start()
    for copy in copies:
        copy.wait()
    position, depth, left = place(axes)
    last_level = axes[2] // 2 - 1
    energy = energy_point(axes)
    on = jnp.concatenate([onsite[0, 0], onsite[0, 1]], axis=1)
    sg = jnp.concatenate([sigma[0, 0, 0], sigma[0, 0, 1]], axis=1)
    h = jnp.concatenate([hopping[0, 0], hopping[0, 1]], axis=1)
    hd = dagger(h)
    h_ref[...] = h
    token_ref[...] = jnp.zeros_like(token_ref)
    hd_ref[...] = hd
    shape = on.shape
    row = lax.broadcasted_iota(jnp.int32, shape, 0)
    column = lax.broadcasted_iota(jnp.int32, shape, 1)
    point = jnp.where(row == column, energy, 0.0) + jnp.where(row + shape[0] == column, BROADEN, 0.0)
    system_ref[...] = point - 0.5 * (on + dagger(on)) - sg

    @pl.when(position == 0)
    def _():
        magnitude = energy * energy + BROADEN * BROADEN
        system_ref[...] = system_ref[...] - times_complex(product(hd, h), energy / magnitude, -BROADEN / magnitude)

    @pl.when(depth == 0)
    def _():
        invert(system_ref[...], green_ref)
        send(left, last_level == 0, green_ref, h, hd, message_ref)

    @pl.when(depth != 0)
    def _():
        green_ref[...] = jnp.zeros(shape, F32)
        message_ref[...] = jnp.zeros(shape, F32)


def send(left, plain, green_ref, h, hd, message_ref):
    if plain:
        message_ref[...] = green_ref[...]
        return

    @pl.when(left)
    def _():
        message_ref[...] = green_ref[...]

    @pl.when(jnp.logical_not(left))
    def _():
        message_ref[...] = product(h, product(green_ref[...], hd))


def inward_kernel(axes, level, _, received, system, green, message, u, v, h, hd, system_ref, green_ref, message_ref, u_ref, v_ref):
    _, depth, left = place(axes)

    @pl.when(depth == level)
    def _():
        got = received[...]

        @pl.when(left)
        def _():
            gh = product(got, h[...])
            u_ref[...] = gh
            v_ref[...] = got
            system_ref[...] = system[...] - product(hd[...], gh)

        @pl.when(jnp.logical_not(left))
        def _():
            system_ref[...] = system[...] - got
            u_ref[...] = u[...]
            v_ref[...] = v[...]

        invert(system_ref[...], green_ref)
        send(left, level == axes[2] // 2 - 1, green_ref, h[...], hd[...], message_ref)

    @pl.when(depth != level)
    def _():
        system_ref[...] = system[...]
        green_ref[...] = green[...]
        message_ref[...] = message[...]
        u_ref[...] = u[...]
        v_ref[...] = v[...]


def middle_kernel(axes, received, system, green, h, hd, following, diagonal_ref, u_ref, token_ref):
    token_ref[...] = jnp.zeros_like(token_ref)
    _, depth, left = place(axes)

    @pl.when(depth == axes[2] // 2 - 1)
    def _():
        got = received[...]
        next_h = following[...]
        right_factor = jnp.where(left, dagger(next_h), h[...])
        left_factor = jnp.where(left, next_h, hd[...])
        gh = product(got, right_factor)
        u_ref[...] = gh
        invert(system[...] - product(left_factor, gh), diagonal_ref)

    @pl.when(depth != axes[2] // 2 - 1)
    def _():
        diagonal_ref[...] = green[...]
        u_ref[...] = jnp.zeros_like(u_ref)


def waiting_kernel(axes, _, received, diagonal, u_in, u_out, outside, h, hd, following, upper_ref, lower_ref, ready_ref):
    position, depth, left = place(axes)
    energy = energy_point(axes)
    magnitude = energy * energy + BROADEN * BROADEN
    contact_re, contact_im = energy / magnitude, -BROADEN / magnitude

    @pl.when(depth == axes[2] // 2 - 1)
    def _():
        u = jnp.where(left, u_out[...], u_in[...])
        v = product(hd[...], jnp.where(left, outside[...], received[...]))
        upper_ref[...] = product(u, diagonal[...])
        lower_ref[...] = product(diagonal[...], v)
        ready_ref[...] = jnp.zeros_like(ready_ref)

    @pl.when(depth != axes[2] // 2 - 1)
    def _():
        g = diagonal[...]
        next_h = following[...]
        right_in = jnp.where(left, dagger(next_h), h[...])
        left_in = jnp.where(left, next_h, hd[...])
        p = product(g, left_in)
        q = product(right_in, g)
        ready_ref[0] = p
        ready_ref[1] = q

        @pl.when(left)
        def _():
            at_contact = position == 0
            u = jnp.where(at_contact, times_complex(h[...], contact_re, contact_im), u_out[...])
            v = jnp.where(at_contact, times_complex(hd[...], contact_re, contact_im), product(hd[...], outside[...]))
            ready_ref[2] = product(u, p)
            ready_ref[3] = product(q, v)
            ready_ref[4] = product(u, g)
            ready_ref[5] = product(g, v)

        upper_ref[...] = jnp.zeros_like(upper_ref)
        lower_ref[...] = jnp.zeros_like(lower_ref)


def outward_kernel(axes, level, final, received, ready, diagonal, upper, lower, *outputs):
    _, depth, left = place(axes)
    if final:
        green_out, packed_ref, green_ref, upper_ref, lower_ref = outputs
    else:
        green_ref, upper_ref, lower_ref = outputs

    @pl.when(depth != level)
    def _():
        green_ref[...] = diagonal[...]
        upper_ref[...] = upper[...]
        lower_ref[...] = lower[...]

    @pl.when(depth == level)
    def _():
        g_in = received[...]
        p = ready[0]
        w = product(g_in, ready[1])
        green_ref[...] = diagonal[...] + product(p, w)

        @pl.when(left)
        def _():
            upper_ref[...] = ready[4] + product(ready[2], w)
            lower_ref[...] = ready[5] + product(p, product(g_in, ready[3]))

        @pl.when(jnp.logical_not(left))
        def _():
            upper_ref[...] = w
            lower_ref[...] = product(p, g_in)

    if final:
        size = diagonal.shape[0]
        blocks = (green_ref[...], upper_ref[...], lower_ref[...])
        for b, block in enumerate(blocks):
            green_out[b, 0] = real_of(block)
            green_out[b, 1] = imag_of(block)
        d0 = blocks[0] - dagger(blocks[0])
        d1 = blocks[1] - dagger(blocks[2])
        row = lax.broadcasted_iota(jnp.int32, (size, size), 0)
        column = lax.broadcasted_iota(jnp.int32, (size, size), 1)
        packed_ref[0] = jnp.where(row > column, real_of(d0), imag_of(d0))
        packed_ref[1] = real_of(d1)
        packed_ref[2] = imag_of(d1)


def unpack(pack, out):
    size = pack.shape[-1]
    row = lax.broadcasted_iota(jnp.int32, (size, size), 0)
    column = lax.broadcasted_iota(jnp.int32, (size, size), 1)
    mixed = pack[0]
    turned = mixed.T
    out[0, 0] = jnp.where(row > column, mixed, jnp.where(row < column, -turned, 0.0))
    out[0, 1] = jnp.where(row > column, turned, mixed)
    out[1] = pack[1:]
    out[2, 0] = -pack[1].T
    out[2, 1] = pack[2].T


def add_term(axes, out, spectral, blocks, index):
    chips, cores, _ = axes
    energy = energy_at(index.astype(F32), chips * cores)
    occupation = 1.0 / (1.0 + jnp.exp(jnp.full((1, 1), energy / THERMAL, F32)))
    for s, scale in enumerate((-occupation, 1.0 - occupation)):
        kernel = blocks(s)
        for b in range(3):
            w_re, w_im = kernel[b, 0], kernel[b, 1]
            g_re, g_im = scale * spectral[b, 0], scale * spectral[b, 1]
            out[s, b, 0] -= g_re * w_im + g_im * w_re
            out[s, b, 1] += g_re * w_re - g_im * w_im


def terms_kernel(axes, same, *refs):
    chips, cores, _ = axes
    packs, rest = refs[:chips], refs[chips:]
    before, spectral, out = rest[0] if not same else None, rest[-1], rest[-2]
    pieces = rest[: len(rest) - 2] if same else rest[1 : len(rest) - 2]
    half = len(pieces) // 2
    own, other = kernel_blocks(chips, pieces[:half]), kernel_blocks(chips, pieces[half:])
    chip, core = lax.axis_index("chip"), lax.axis_index("core")
    out[...] = jnp.zeros_like(out) if same else before[...]
    for r in range(chips):
        @pl.when(chip >= r)
        def _():
            unpack(packs[r], spectral.at[r])
    for offset in range(chips):
        chip_of = jnp.bitwise_xor(chip, offset) if len(pieces) > 2 else jnp.int32(offset)
        for c in range(cores):
            r = chip_of if same else chip_of + 1 - c
            source = (own if c == 0 else other) if same else (other if c == 0 else own)
            origin = core if same else 1 - core

            @pl.when(jnp.logical_and(core == c, r <= chip))
            def _():
                blocks = functools.partial(source[offset], chip_of)
                add_term(axes, out, spectral.at[r], blocks, (chip - r) * cores + origin)


class Exchange:
    def __init__(self, chips, cores, screened):
        self.paired = chips == 4
        self.swap = [(i, i ^ 1) for i in range(cores)] if cores == 2 else []
        self.own = screened[0, 0]
        self.early = []
        self.pieces = [self.own] if self.paired else [lax.all_gather(self.own, "chip", axis=0)]

    def moved(self, piece, offset):
        return lax.ppermute(piece, "chip", [(i, i ^ offset) for i in range(4)])

    def begin(self, after):
        if self.paired:
            own, _ = lax.optimization_barrier((self.own, after))
            self.pieces += [self.moved(own, 1), self.moved(own, 2)]

    def go_on(self, after):
        if self.paired:
            one, two = self.pieces[1:]
            one, two, _ = lax.optimization_barrier((one, two, after))
            self.pieces += [self.moved(one[:1], 2), self.moved(two[1:], 1)]
            own, one, two, _ = lax.optimization_barrier((*self.pieces[:3], after))
            self.early = [lax.ppermute(piece, "core", self.swap) for piece in (own, one, two)]

    def finish(self, after):
        late = self.pieces[3:] if self.paired else self.pieces
        *late, _ = lax.optimization_barrier((*late, after))
        return self.pieces, self.early + [lax.ppermute(piece, "core", self.swap) for piece in late]


def kernel_blocks(chips, pieces):
    if len(pieces) == 1:
        return [(lambda chip_of, kind: pieces[0].at[chip_of, kind])] * chips
    found = [(lambda chip_of, kind, piece=piece: piece.at[kind]) for piece in pieces[:3]]
    return found + [lambda chip_of, kind: pieces[3 + kind].at[0]]


def local(axes, onsite, hopping, sigma_old, screened):
    chips, cores, cells_all = axes
    size = sigma_old.shape[-1]
    half = cells_all // 2
    matrix = jax.ShapeDtypeStruct((size, 2 * size), F32)
    def call(body, out_shape, *operands, space=pltpu.VMEM, grant=16, work=WORK, **options):
        spec = pl.BlockSpec(memory_space=pltpu.VMEM)
        return pl.pallas_call(
            functools.partial(body, axes),
            out_shape=out_shape,
            in_specs=[pl.BlockSpec(memory_space=space)] * len(operands),
            out_specs=jax.tree.map(lambda _: spec, out_shape),
            compiler_params=pltpu.CompilerParams(vmem_limit_bytes=grant * 1024 * 1024),
            cost_estimate=pl.CostEstimate(
                flops=int(work * 80 * (2 * size) ** 3), bytes_accessed=2 * 1024 * 1024, transcendentals=0
            ),
            **options,
        )(*operands)

    swap = [(i, i ^ 1) for i in range(cores)] if cores == 2 else []
    exchange = Exchange(chips, cores, screened)
    token = jax.ShapeDtypeStruct((8, size), F32)
    system, green, message, h, hd, mark = call(
        outer_kernel,
        (matrix,) * 5 + (token,),
        *(pltpu.with_memory_space_constraint(a, pltpu.HBM) for a in (onsite, hopping, sigma_old)),
        space=pltpu.HBM,
        scratch_shapes=[pltpu.VMEM(a.shape, F32) for a in (onsite, hopping, sigma_old)]
        + [pltpu.SemaphoreType.DMA((3,))],
    )
    mark = lax.ppermute(mark, "core", swap)
    exchange.begin(mark)
    h_sent, _ = lax.optimization_barrier((h, mark))
    following = lax.ppermute(h_sent, "space", [(i + 1, i) for i in range(cells_all - 1)])
    u_out = outside = jnp.zeros((size, 2 * size), F32)
    for level in range(1, half):
        route = [(level - 1, level), (cells_all - level, cells_all - 1 - level)]
        received = lax.ppermute(message, "space", route)
        if level == 1:
            received, following = lax.optimization_barrier((received, following))
        system, green, message, u_out, outside = call(
            functools.partial(swapped, inward_kernel, level),
            (matrix,) * 5,
            mark, received, system, green, message, u_out, outside, h, hd,
            work=WORK2,
        )
    received = lax.ppermute(message, "space", [(half - 1, half), (half, half - 1)])
    diagonal, u_in, mark = call(
        middle_kernel, (matrix,) * 2 + (token,), received, system, green, h, hd, following,
        work=WORK3,
    )
    mark = lax.ppermute(mark, "core", swap)
    exchange.go_on(mark)
    upper = None
    for level in reversed(range(half - 1)):
        route = [(level + 1, level), (cells_all - 2 - level, cells_all - 1 - level)]
        arrived = lax.ppermute(diagonal, "space", route)
        if upper is None:
            upper, lower, ready = call(
                waiting_kernel,
                (matrix, matrix, jax.ShapeDtypeStruct((6, size, 2 * size), F32)),
                mark, received, diagonal, u_in, u_out, outside, h, hd, following,
                work=WORK4,
            )
        final = level == 0
        shapes = (matrix,) * 3
        if final:
            shapes = (
                jax.ShapeDtypeStruct((3, 2, size, size), F32),
                jax.ShapeDtypeStruct((3, size, size), F32),
            ) + shapes
        results = call(
            functools.partial(swapped, outward_kernel, level, final),
            shapes,
            arrived, ready, diagonal, upper, lower,
            work=WORK6,
        )
        diagonal, upper, lower = results[-3:]
    green_out, packed = results[:2]
    own = [packed] + [
        lax.ppermute(packed, "chip", [(i, i + r) for i in range(chips - r)]) for r in range(1, chips)
    ]
    if exchange.paired:
        *arrived, exchange.pieces[3], exchange.pieces[4] = lax.optimization_barrier((*own[1:], *exchange.pieces[3:]))
        own[1:] = arrived
    other = [lax.ppermute(pack, "core", swap) for pack in own]
    pieces, other_pieces = exchange.finish(own[1:] if chips > 1 else packed)
    result = jax.ShapeDtypeStruct((2, 3, 2, size, size), F32)
    unpacked = [pltpu.VMEM((chips, 3, 2, size, size), F32)]
    partial = call(
        functools.partial(swapped, terms_kernel, True), result, *own, *pieces, *other_pieces,
        scratch_shapes=unpacked,
        work=WORK5,
    )
    sigma_out = call(
        functools.partial(swapped, terms_kernel, False), result, *other, partial, *pieces, *other_pieces,
        scratch_shapes=unpacked,
    )
    return green_out[None, None], sigma_out[None, None]


def swapped(body, *arguments):
    fixed = [a for a in arguments if isinstance(a, (int, bool))]
    axes, *refs = arguments[len(fixed) :]
    return body(axes, *fixed, *refs)


def solution(mesh):
    cores = 2 if mesh.shape["energy"] % 2 == 0 else 1
    axes = (mesh.shape["energy"] // cores, cores, mesh.shape["space"])
    split_mesh = jax.sharding.Mesh(mesh.devices.reshape(axes), ("chip", "core", "space"))
    energy = ("chip", "core")
    placed = (
        P("space", None, None, None),
        P("space", None, None, None),
        P(energy, "space", None, None, None),
        P(energy, "space", None, None, None, None, None),
    )
    return jax.shard_map(
        functools.partial(local, axes),
        mesh=split_mesh,
        in_specs=placed,
        out_specs=(
            P(energy, "space", None, None, None, None),
            P(energy, "space", None, None, None, None, None),
        ),
        check_vma=False,
    )
```

profile of v0, /device:TPU:0, one launch (start us, length us, event | category | flops | bytes accessed | tf_op | source)
XLA Modules:
  0.0 63.0 jit_solution(13741429482682728982)
XLA Ops:
  0.6 3.9 %shard_map.59 = (f32[128,256]{1,0:T(8,128)S(1)}, f32[128,256]{1,0:T(8,128)S(1)}, f32[128,256]{1,0:T(8,128)S(1)}, f32[128,256]{1,0:T(8,128)S(1)}, f32[128,256]{1,0:T(8,128)S(1)}, /*index=5*/f32[8,128]{1,0:T(8,128)S(1)}) custom-call(f32[1,2,128,128]{3,2,1,0:T(8,128)} %onsite_far.1, f32[1,2,128,128]{3,2,1,0:T(8,128)} %hopping_far.1, ...), custom_call_target="tpu_custom_call" | custom-call | flops 1342177280 | bytes 2097152 | tf_op jit(solution)/shard_map/pallas_call | solution.py:449
  4.5 0.5 collective-permute-start
  5.0 1.9 %collective-permute-start.1 = (f32[128,256]{1,0:T(8,128)S(1)}, f32[128,256]{1,0:T(8,128)S(1)}, u32[]{:S(2)}, u32[]{:S(2)}) collective-permute-start(f32[128,256]{1,0:T(8,128)S(1)} %get-tuple-element.38.arguments_4_), channel_id=1, source_target_pairs={{0,1},{3,2},{4,5},{7,6},{8,9},{11,10},{12,13},{15,14},{16,17},{19,... | collective-permute-start | bytes 393224 | tf_op jit(solution)/shard_map/ppermute | solution.py:479
  7.0 1.3 %collective-permute-start.2 = (f32[128,256]{1,0:T(8,128)S(1)}, f32[128,256]{1,0:T(8,128)S(1)}, u32[]{:S(2)}, u32[]{:S(2)}) collective-permute-start(f32[128,256]{1,0:T(8,128)S(1)} %get-tuple-element.40.arguments_7_.h), channel_id=1, source_target_pairs={{1,0},{2,1},{3,2},{5,4},{6,5},{7,6},{9,8},{10,9},{11,10},{13,12},{... | collective-permute-start | bytes 393224 | tf_op jit(solution)/shard_map/ppermute | solution.py:475
  8.3 2.0 %collective-permute-start.11 = (f32[2,3,2,128,128]{4,3,2,1,0:T(8,128)S(1)}, f32[2,3,2,128,128]{4,3,2,1,0:T(8,128)S(1)}, u32[]{:S(2)}, u32[]{:S(2)}) collective-permute-start(f32[2,3,2,128,128]{4,3,2,1,0:T(8,128)S(1)} %bitcast.3), channel_id=1, source_target_pairs={{0,16},{8,24},{16,0},{24,8},{1,17},{9,25},{17,1},{25,9},{2,18},{10... | collective-permute-start | bytes 2359304 | tf_op jit(solution)/shard_map/ppermute | solution.py:414
  10.2 1.5 %collective-permute-start.10 = (f32[2,3,2,128,128]{4,3,2,1,0:T(8,128)S(1)}, f32[2,3,2,128,128]{4,3,2,1,0:T(8,128)S(1)}, u32[]{:S(2)}, u32[]{:S(2)}) collective-permute-start(f32[2,3,2,128,128]{4,3,2,1,0:T(8,128)S(1)} %bitcast.4), channel_id=1, source_target_pairs={{0,8},{8,0},{16,24},{24,16},{1,9},{9,1},{17,25},{25,17},{2,10},{10... | collective-permute-start | bytes 2359304 | tf_op jit(solution)/shard_map/ppermute | solution.py:414
  11.7 2.7 %collective-permute-done.2.following = f32[128,256]{1,0:T(8,128)S(1)} collective-permute-done((f32[128,256]{1,0:T(8,128)S(1)}, f32[128,256]{1,0:T(8,128)S(1)}, u32[]{:S(2)}, u32[]{:S(2)}) %collective-permute-start.2) | collective-permute-done | bytes 131104 | tf_op jit(solution)/shard_map/ppermute | solution.py:475
  14.6 0.7 %collective-permute-start.3 = (f32[128,256]{1,0:T(8,128)S(1)}, f32[128,256]{1,0:T(8,128)S(1)}, u32[]{:S(2)}, u32[]{:S(2)}) collective-permute-start(f32[128,256]{1,0:T(8,128)S(1)} %get-tuple-element.45), channel_id=1, source_target_pairs={{1,2},{2,1},{5,6},{6,5},{9,10},{10,9},{13,14},{14,13},{17,18},{18,... | collective-permute-start | bytes 393224 | tf_op jit(solution)/shard_map/ppermute | solution.py:488
  15.3 1.3 %collective-permute-start.4 = (f32[128,256]{1,0:T(8,128)S(1)}, f32[128,256]{1,0:T(8,128)S(1)}, u32[]{:S(2)}, u32[]{:S(2)}) collective-permute-start(f32[128,256]{1,0:T(8,128)S(1)} %get-tuple-element.49.diagonal.arguments_2_), channel_id=1, source_target_pairs={{1,0},{2,3},{5,4},{6,7},{9,8},{10,11},{13,12},{14,15},{17,16},{18,... | collective-permute-start | bytes 393224 | tf_op jit(solution)/shard_map/ppermute | solution.py:498
  16.7 1.2 %collective-permute-done.5._ = f32[8,128]{1,0:T(8,128)S(1)} collective-permute-done((f32[8,128]{1,0:T(8,128)S(1)}, f32[8,128]{1,0:T(8,128)S(1)}, u32[]{:S(2)}, u32[]{:S(2)}) %collective-permute-start.5) | collective-permute-done | bytes 4128 | tf_op jit(solution)/shard_map/ppermute | solution.py:493
  17.8 0.9 %shard_map.62 = (f32[128,256]{1,0:T(8,128)S(1)}, f32[128,256]{1,0:T(8,128)S(1)}, f32[6,128,256]{2,1,0:T(8,128)S(1)}) custom-call(f32[8,128]{1,0:T(8,128)S(1)} %collective-permute-done.5._, f32[128,256]{1,0:T(8,128)S(1)} %collective-permute-done.3.received, f32[128,256]{1,0:T(8,128)S(1)} %get-tuple-element.49.diagonal.arguments_2_, ...), custom_call_target="tpu_custom_call" | custom-call | flops 1342177280 | bytes 2097152 | tf_op jit(solution)/shard_map/pallas_call | solution.py:449
  18.8 15.6 %collective-permute-done.4.arguments_0_ = f32[128,256]{1,0:T(8,128)S(1)} collective-permute-done((f32[128,256]{1,0:T(8,128)S(1)}, f32[128,256]{1,0:T(8,128)S(1)}, u32[]{:S(2)}, u32[]{:S(2)}) %collective-permute-start.4) | collective-permute-done | bytes 131104 | tf_op jit(solution)/shard_map/ppermute | solution.py:498
  34.4 1.9 %shard_map.63 = (f32[3,2,128,128]{3,2,1,0:T(8,128)}, f32[3,128,128]{2,1,0:T(8,128)S(1)}, f32[128,256]{1,0:T(8,128)}, f32[128,256]{1,0:T(8,128)}, f32[128,256]{1,0:T(8,128)}) custom-call(f32[128,256]{1,0:T(8,128)S(1)} %collective-permute-done.4.arguments_0_, f32[6,128,256]{2,1,0:T(8,128)S(1)} %get-tuple-element.54.arguments_1_, ...), custom_call_target="tpu_custom_call" | custom-call | flops 1342177280 | bytes 2097152 | tf_op jit(solution)/shard_map/pallas_call | solution.py:449
  36.3 4.3 %collective-permute-start.9 = (f32[3,128,128]{2,1,0:T(8,128)S(1)}, f32[3,128,128]{2,1,0:T(8,128)S(1)}, u32[]{:S(2)}, u32[]{:S(2)}) collective-permute-start(f32[3,128,128]{2,1,0:T(8,128)S(1)} %get-tuple-element.58.arguments_0_), channel_id=1, source_target_pairs={{0,24},{1,25},{2,26},{3,27},{4,28},{5,29},{6,30},{7,31}} | collective-permute-start | bytes 589832 | tf_op jit(solution)/shard_map/ppermute | solution.py:522
  40.6 1.3 %collective-permute-start.8 = (f32[3,128,128]{2,1,0:T(8,128)S(1)}, f32[3,128,128]{2,1,0:T(8,128)S(1)}, u32[]{:S(2)}, u32[]{:S(2)}) collective-permute-start(f32[3,128,128]{2,1,0:T(8,128)S(1)} %get-tuple-element.58.arguments_0_), channel_id=1, source_target_pairs={{0,16},{8,24},{1,17},{9,25},{2,18},{10,26},{3,19},{11,27},{4,20},{... | collective-permute-start | bytes 589832 | tf_op jit(solution)/shard_map/ppermute | solution.py:522
  42.0 2.5 %collective-permute-start.7 = (f32[3,128,128]{2,1,0:T(8,128)S(1)}, f32[3,128,128]{2,1,0:T(8,128)S(1)}, u32[]{:S(2)}, u32[]{:S(2)}) collective-permute-start(f32[3,128,128]{2,1,0:T(8,128)S(1)} %get-tuple-element.58.arguments_0_), channel_id=1, source_target_pairs={{0,8},{8,16},{16,24},{1,9},{9,17},{17,25},{2,10},{10,18},{18,26},{... | collective-permute-start | bytes 589832 | tf_op jit(solution)/shard_map/ppermute | solution.py:522
  44.8 6.5 %collective-permute-done.8.arguments_2_ = f32[3,128,128]{2,1,0:T(8,128)S(1)} collective-permute-done((f32[3,128,128]{2,1,0:T(8,128)S(1)}, f32[3,128,128]{2,1,0:T(8,128)S(1)}, u32[]{:S(2)}, u32[]{:S(2)}) %collective-permute-start.8) | collective-permute-done | bytes 196640 | tf_op jit(solution)/shard_map/ppermute | solution.py:522
  51.3 0.5 collective-permute-start.19
  51.8 4.6 %collective-permute-done.13.arguments_8_.arguments_9_ = f32[1,3,2,128,128]{4,3,2,1,0:T(8,128)S(1)} collective-permute-done((f32[1,3,2,128,128]{4,3,2,1,0:T(8,128)S(1)}, f32[1,3,2,128,128]{4,3,2,1,0:T(8,128)S(1)}, u32[]{:S(2)}, u32[]{:S(2)}) %collective-permute-start.13) | collective-permute-done | bytes 393248 | tf_op jit(solution)/shard_map/ppermute | solution.py:414
  56.4 1.2 %collective-permute-done.12.arguments_7_.arguments_8_ = f32[1,3,2,128,128]{4,3,2,1,0:T(8,128)S(1)} collective-permute-done((f32[1,3,2,128,128]{4,3,2,1,0:T(8,128)S(1)}, f32[1,3,2,128,128]{4,3,2,1,0:T(8,128)S(1)}, u32[]{:S(2)}, u32[]{:S(2)}) %collective-permute-start.12) | collective-permute-done | bytes 393248 | tf_op jit(solution)/shard_map/ppermute | solution.py:414
  57.6 0.5 collective-permute-start.21
  58.1 1.2 %collective-permute-done.20.arguments_12_.arguments_13_ = f32[1,3,2,128,128]{4,3,2,1,0:T(8,128)S(1)} collective-permute-done((f32[1,3,2,128,128]{4,3,2,1,0:T(8,128)S(1)}, f32[1,3,2,128,128]{4,3,2,1,0:T(8,128)S(1)}, u32[]{:S(2)}, u32[]{:S(2)}) %collective-permute-start.20) | collective-permute-done | bytes 393248 | tf_op jit(solution)/shard_map/ppermute | solution.py:432
  59.5 0.4 collective-permute-done.21.arguments_13_.arguments_14_
  61.9 1.1 %shard_map.65 = f32[2,3,2,128,128]{4,3,2,1,0:T(8,128)} custom-call(f32[3,128,128]{2,1,0:T(8,128)S(1)} %collective-permute-done.6.arguments_0_, f32[3,128,128]{2,1,0:T(8,128)S(1)} %collective-permute-done.14.arguments_1_, f32[3,128,128]{2,1,0:T(8,128)S(1)} %collective-permute-done.15.arguments_2_, f32[3,128,128]{2,1,0:T(8,128)S(1)} %collective-permute-done.16.arguments_3_, ...), custom_call_target="tpu_custom_call" | custom-call | flops 1342177280 | bytes 2097152 | tf_op jit(solution)/shard_map/pallas_call | solution.py:449
  (32 shorter events, 2.6 us)
Async XLA Ops:
  0.6 7.6 %copy-start = (f32[1,1,2,3,2,128,128]{6,5,4,3,2,1,0:T(8,128)S(1)}, f32[1,1,2,3,2,128,128]{6,5,4,3,2,1,0:T(8,128)}, u32[]{:S(2)}) copy-start(f32[1,1,2,3,2,128,128]{6,5,4,3,2,1,0:T(8,128)} %param.7) | copy-start | bytes 2359300
  4.5 2.5 %collective-permute-start = (f32[8,128]{1,0:T(8,128)S(1)}, f32[8,128]{1,0:T(8,128)S(1)}, u32[]{:S(2)}, u32[]{:S(2)}) collective-permute-start(f32[8,128]{1,0:T(8,128)S(1)} %get-tuple-element.37), channel_id=1, source_target_pairs={{0,4},{4,0},{1,5},{5,1},{2,6},{6,2},{3,7},{7,3},{8,12},{12,8},{9,1... | collective-permute-start | bytes 12296 | tf_op jit(solution)/shard_map/ppermute | solution.py:472
  5.0 6.7 %collective-permute-start.1 = (f32[128,256]{1,0:T(8,128)S(1)}, f32[128,256]{1,0:T(8,128)S(1)}, u32[]{:S(2)}, u32[]{:S(2)}) collective-permute-start(f32[128,256]{1,0:T(8,128)S(1)} %get-tuple-element.38.arguments_4_), channel_id=1, source_target_pairs={{0,1},{3,2},{4,5},{7,6},{8,9},{11,10},{12,13},{15,14},{16,17},{19,... | collective-permute-start | bytes 393224 | tf_op jit(solution)/shard_map/ppermute | solution.py:479
  7.0 7.5 %collective-permute-start.2 = (f32[128,256]{1,0:T(8,128)S(1)}, f32[128,256]{1,0:T(8,128)S(1)}, u32[]{:S(2)}, u32[]{:S(2)}) collective-permute-start(f32[128,256]{1,0:T(8,128)S(1)} %get-tuple-element.40.arguments_7_.h), channel_id=1, source_target_pairs={{1,0},{2,1},{3,2},{5,4},{6,5},{7,6},{9,8},{10,9},{11,10},{13,12},{... | collective-permute-start | bytes 393224 | tf_op jit(solution)/shard_map/ppermute | solution.py:475
  8.3 36.2 %collective-permute-start.11 = (f32[2,3,2,128,128]{4,3,2,1,0:T(8,128)S(1)}, f32[2,3,2,128,128]{4,3,2,1,0:T(8,128)S(1)}, u32[]{:S(2)}, u32[]{:S(2)}) collective-permute-start(f32[2,3,2,128,128]{4,3,2,1,0:T(8,128)S(1)} %bitcast.3), channel_id=1, source_target_pairs={{0,16},{8,24},{16,0},{24,8},{1,17},{9,25},{17,1},{25,9},{2,18},{10... | collective-permute-start | bytes 2359304 | tf_op jit(solution)/shard_map/ppermute | solution.py:414
  10.2 34.2 %collective-permute-start.10 = (f32[2,3,2,128,128]{4,3,2,1,0:T(8,128)S(1)}, f32[2,3,2,128,128]{4,3,2,1,0:T(8,128)S(1)}, u32[]{:S(2)}, u32[]{:S(2)}) collective-permute-start(f32[2,3,2,128,128]{4,3,2,1,0:T(8,128)S(1)} %bitcast.4), channel_id=1, source_target_pairs={{0,8},{8,0},{16,24},{24,16},{1,9},{9,1},{17,25},{25,17},{2,10},{10... | collective-permute-start | bytes 2359304 | tf_op jit(solution)/shard_map/ppermute | solution.py:414
  14.6 0.7 %collective-permute-start.3 = (f32[128,256]{1,0:T(8,128)S(1)}, f32[128,256]{1,0:T(8,128)S(1)}, u32[]{:S(2)}, u32[]{:S(2)}) collective-permute-start(f32[128,256]{1,0:T(8,128)S(1)} %get-tuple-element.45), channel_id=1, source_target_pairs={{1,2},{2,1},{5,6},{6,5},{9,10},{10,9},{13,14},{14,13},{17,18},{18,... | collective-permute-start | bytes 393224 | tf_op jit(solution)/shard_map/ppermute | solution.py:488
  15.3 19.1 %collective-permute-start.4 = (f32[128,256]{1,0:T(8,128)S(1)}, f32[128,256]{1,0:T(8,128)S(1)}, u32[]{:S(2)}, u32[]{:S(2)}) collective-permute-start(f32[128,256]{1,0:T(8,128)S(1)} %get-tuple-element.49.diagonal.arguments_2_), channel_id=1, source_target_pairs={{1,0},{2,3},{5,4},{6,7},{9,8},{10,11},{13,12},{14,15},{17,16},{18,... | collective-permute-start | bytes 393224 | tf_op jit(solution)/shard_map/ppermute | solution.py:498
  16.6 1.2 %collective-permute-start.5 = (f32[8,128]{1,0:T(8,128)S(1)}, f32[8,128]{1,0:T(8,128)S(1)}, u32[]{:S(2)}, u32[]{:S(2)}) collective-permute-start(f32[8,128]{1,0:T(8,128)S(1)} %get-tuple-element.50), channel_id=1, source_target_pairs={{0,4},{4,0},{1,5},{5,1},{2,6},{6,2},{3,7},{7,3},{8,12},{12,8},{9,1... | collective-permute-start | bytes 12296 | tf_op jit(solution)/shard_map/ppermute | solution.py:493
  36.3 8.4 %collective-permute-start.9 = (f32[3,128,128]{2,1,0:T(8,128)S(1)}, f32[3,128,128]{2,1,0:T(8,128)S(1)}, u32[]{:S(2)}, u32[]{:S(2)}) collective-permute-start(f32[3,128,128]{2,1,0:T(8,128)S(1)} %get-tuple-element.58.arguments_0_), channel_id=1, source_target_pairs={{0,24},{1,25},{2,26},{3,27},{4,28},{5,29},{6,30},{7,31}} | collective-permute-start | bytes 589832 | tf_op jit(solution)/shard_map/ppermute | solution.py:522
  40.6 10.7 %collective-permute-start.8 = (f32[3,128,128]{2,1,0:T(8,128)S(1)}, f32[3,128,128]{2,1,0:T(8,128)S(1)}, u32[]{:S(2)}, u32[]{:S(2)}) collective-permute-start(f32[3,128,128]{2,1,0:T(8,128)S(1)} %get-tuple-element.58.arguments_0_), channel_id=1, source_target_pairs={{0,16},{8,24},{1,17},{9,25},{2,18},{10,26},{3,19},{11,27},{4,20},{... | collective-permute-start | bytes 589832 | tf_op jit(solution)/shard_map/ppermute | solution.py:522
  42.0 9.3 %collective-permute-start.7 = (f32[3,128,128]{2,1,0:T(8,128)S(1)}, f32[3,128,128]{2,1,0:T(8,128)S(1)}, u32[]{:S(2)}, u32[]{:S(2)}) collective-permute-start(f32[3,128,128]{2,1,0:T(8,128)S(1)} %get-tuple-element.58.arguments_0_), channel_id=1, source_target_pairs={{0,8},{8,16},{16,24},{1,9},{9,17},{17,25},{2,10},{10,18},{18,26},{... | collective-permute-start | bytes 589832 | tf_op jit(solution)/shard_map/ppermute | solution.py:522
  44.5 11.9 %collective-permute-start.13 = (f32[1,3,2,128,128]{4,3,2,1,0:T(8,128)S(1)}, f32[1,3,2,128,128]{4,3,2,1,0:T(8,128)S(1)}, u32[]{:S(2)}, u32[]{:S(2)}) collective-permute-start(f32[1,3,2,128,128]{4,3,2,1,0:T(8,128)S(1)} %slice.7), channel_id=1, source_target_pairs={{0,8},{8,0},{16,24},{24,16},{1,9},{9,1},{17,25},{25,17},{2,10},{10... | collective-permute-start | bytes 1179656 | tf_op jit(solution)/shard_map/ppermute | solution.py:414
  44.6 13.0 %collective-permute-start.12 = (f32[1,3,2,128,128]{4,3,2,1,0:T(8,128)S(1)}, f32[1,3,2,128,128]{4,3,2,1,0:T(8,128)S(1)}, u32[]{:S(2)}, u32[]{:S(2)}) collective-permute-start(f32[1,3,2,128,128]{4,3,2,1,0:T(8,128)S(1)} %slice.6), channel_id=1, source_target_pairs={{0,16},{8,24},{16,0},{24,8},{1,17},{9,25},{17,1},{25,9},{2,18},{10... | collective-permute-start | bytes 1179656 | tf_op jit(solution)/shard_map/ppermute | solution.py:414
  44.7 15.4 %collective-permute-start.17 = (f32[2,3,2,128,128]{4,3,2,1,0:T(8,128)S(1)}, f32[2,3,2,128,128]{4,3,2,1,0:T(8,128)S(1)}, u32[]{:S(2)}, u32[]{:S(2)}) collective-permute-start(f32[2,3,2,128,128]{4,3,2,1,0:T(8,128)S(1)} %bitcast.5), channel_id=1, source_target_pairs={{0,4},{4,0},{1,5},{5,1},{2,6},{6,2},{3,7},{7,3},{8,12},{12,8},{9,1... | collective-permute-start | bytes 2359304 | tf_op jit(solution)/shard_map/ppermute | solution.py:427
  51.3 9.1 %collective-permute-start.18 = (f32[2,3,2,128,128]{4,3,2,1,0:T(8,128)S(1)}, f32[2,3,2,128,128]{4,3,2,1,0:T(8,128)S(1)}, u32[]{:S(2)}, u32[]{:S(2)}) collective-permute-start(f32[2,3,2,128,128]{4,3,2,1,0:T(8,128)S(1)} %collective-permute-done.10.arguments_5_.arguments_6_), channel_id=1, source_target_pairs={{0,4},{4,0},{1,5},{5,1},{2,6},{6,2},{3,7},{7,3},{8,12},{12,8},{9,1... | collective-permute-start | bytes 2359304 | tf_op jit(solution)/shard_map/ppermute | solution.py:427
  51.3 9.3 %collective-permute-start.19 = (f32[2,3,2,128,128]{4,3,2,1,0:T(8,128)S(1)}, f32[2,3,2,128,128]{4,3,2,1,0:T(8,128)S(1)}, u32[]{:S(2)}, u32[]{:S(2)}) collective-permute-start(f32[2,3,2,128,128]{4,3,2,1,0:T(8,128)S(1)} %collective-permute-done.11.arguments_6_.arguments_7_), channel_id=1, source_target_pairs={{0,4},{4,0},{1,5},{5,1},{2,6},{6,2},{3,7},{7,3},{8,12},{12,8},{9,1... | collective-permute-start | bytes 2359304 | tf_op jit(solution)/shard_map/ppermute | solution.py:427
  57.6 1.7 %collective-permute-start.20 = (f32[1,3,2,128,128]{4,3,2,1,0:T(8,128)S(1)}, f32[1,3,2,128,128]{4,3,2,1,0:T(8,128)S(1)}, u32[]{:S(2)}, u32[]{:S(2)}) collective-permute-start(f32[1,3,2,128,128]{4,3,2,1,0:T(8,128)S(1)} %collective-permute-done.12.arguments_7_.arguments_8_), channel_id=1, source_target_pairs={{0,4},{4,0},{1,5},{5,1},{2,6},{6,2},{3,7},{7,3},{8,12},{12,8},{9,1... | collective-permute-start | bytes 1179656 | tf_op jit(solution)/shard_map/ppermute | solution.py:432
  57.6 2.3 %collective-permute-start.21 = (f32[1,3,2,128,128]{4,3,2,1,0:T(8,128)S(1)}, f32[1,3,2,128,128]{4,3,2,1,0:T(8,128)S(1)}, u32[]{:S(2)}, u32[]{:S(2)}) collective-permute-start(f32[1,3,2,128,128]{4,3,2,1,0:T(8,128)S(1)} %collective-permute-done.13.arguments_8_.arguments_9_), channel_id=1, source_target_pairs={{0,4},{4,0},{1,5},{5,1},{2,6},{6,2},{3,7},{7,3},{8,12},{12,8},{9,1... | collective-permute-start | bytes 1179656 | tf_op jit(solution)/shard_map/ppermute | solution.py:432
  59.4 1.6 %collective-permute-start.6 = (f32[3,128,128]{2,1,0:T(8,128)S(1)}, f32[3,128,128]{2,1,0:T(8,128)S(1)}, u32[]{:S(2)}, u32[]{:S(2)}) collective-permute-start(f32[3,128,128]{2,1,0:T(8,128)S(1)} %get-tuple-element.58.arguments_0_), channel_id=1, source_target_pairs={{0,4},{4,0},{1,5},{5,1},{2,6},{6,2},{3,7},{7,3},{8,12},{12,8},{9,1... | collective-permute-start | bytes 589832 | tf_op jit(solution)/shard_map/ppermute | solution.py:527
  59.9 1.4 %collective-permute-start.14 = (f32[3,128,128]{2,1,0:T(8,128)S(1)}, f32[3,128,128]{2,1,0:T(8,128)S(1)}, u32[]{:S(2)}, u32[]{:S(2)}) collective-permute-start(f32[3,128,128]{2,1,0:T(8,128)S(1)} %collective-permute-done.7.arguments_1_), channel_id=1, source_target_pairs={{0,4},{4,0},{1,5},{5,1},{2,6},{6,2},{3,7},{7,3},{8,12},{12,8},{9,1... | collective-permute-start | bytes 589832 | tf_op jit(solution)/shard_map/ppermute | solution.py:527
  60.1 1.6 %collective-permute-start.15 = (f32[3,128,128]{2,1,0:T(8,128)S(1)}, f32[3,128,128]{2,1,0:T(8,128)S(1)}, u32[]{:S(2)}, u32[]{:S(2)}) collective-permute-start(f32[3,128,128]{2,1,0:T(8,128)S(1)} %collective-permute-done.8.arguments_2_), channel_id=1, source_target_pairs={{0,4},{4,0},{1,5},{5,1},{2,6},{6,2},{3,7},{7,3},{8,12},{12,8},{9,1... | collective-permute-start | bytes 589832 | tf_op jit(solution)/shard_map/ppermute | solution.py:527
  60.4 1.5 %collective-permute-start.16 = (f32[3,128,128]{2,1,0:T(8,128)S(1)}, f32[3,128,128]{2,1,0:T(8,128)S(1)}, u32[]{:S(2)}, u32[]{:S(2)}) collective-permute-start(f32[3,128,128]{2,1,0:T(8,128)S(1)} %collective-permute-done.9.arguments_3_), channel_id=1, source_target_pairs={{0,4},{4,0},{1,5},{5,1},{2,6},{6,2},{3,7},{7,3},{8,12},{12,8},{9,1... | collective-permute-start | bytes 589832 | tf_op jit(solution)/shard_map/ppermute | solution.py:527
where the time goes:
time: 63.9 us; the launch traced here: 63 us
  waiting for transfers between devices  34.5 us (54%)
  starting transfers between devices  19.4 us (30%)
  Pallas kernels  8.28 us (13%)
  between operations  0.85 us (1%)
    ppermute x1, waiting for transfers between devices, local(): arrived = lax.ppermute(diagonal, 'space', route)  15.6 us
    pallas_call x7, Pallas kernels, call(): pl.pallas_call(functools.partial(body, axes), out_shape=out_shape, in_spe...  8.28 us
    ppermute x3, starting transfers between devices, local(): lax.ppermute(packed, 'chip', [(i, i + r) for i in range(chips - r)])  8.12 us
    ppermute x3, waiting for transfers between devices, local(): lax.ppermute(packed, 'chip', [(i, i + r) for i in range(chips - r)])  6.53 us
    ppermute x4, waiting for transfers between devices, moved(): return lax.ppermute(piece, 'chip', [(i, i ^ offset) for i in range(4)])  5.83 us
    ppermute x4, starting transfers between devices, moved(): return lax.ppermute(piece, 'chip', [(i, i ^ offset) for i in range(4)])  3.6 us
    ppermute x1, waiting for transfers between devices, local(): lax.ppermute(h_sent, 'space', [(i + 1, i) for i in range(cells_all - 1)])  2.73 us
    ppermute x1, starting transfers between devices, local(): received = lax.ppermute(message, 'space', route)  1.93 us
  transfers between devices with their start and end apart: 22, of which 11 were waited for; matrix products, arithmetic and copies ran while one was open for 0% of the time, Pallas kernels for 5%

commit v1 on v0

--- a/solution.py
+++ b/solution.py
@@ -169,7 +169,6 @@
     for copy in copies:
         copy.wait()
     position, depth, left = place(axes)
-    last_level = axes[2] // 2 - 1
     energy = energy_point(axes)
     on = jnp.concatenate([onsite[0, 0], onsite[0, 1]], axis=1)
     sg = jnp.concatenate([sigma[0, 0, 0], sigma[0, 0, 1]], axis=1)
@@ -192,7 +191,7 @@
     @pl.when(depth == 0)
     def _():
         invert(system_ref[...], green_ref)
-        send(left, last_level == 0, green_ref, h, hd, message_ref)
+        send(left, green_ref, h, hd, message_ref)
 
     @pl.when(depth != 0)
     def _():
@@ -200,21 +199,17 @@
         message_ref[...] = jnp.zeros(shape, F32)
 
 
-def send(left, plain, green_ref, h, hd, message_ref):
-    if plain:
+def send(plain, green_ref, h, hd, message_ref):
+    @pl.when(plain)
+    def _():
         message_ref[...] = green_ref[...]
-        return
-
-    @pl.when(left)
-    def _():
-        message_ref[...] = green_ref[...]
-
-    @pl.when(jnp.logical_not(left))
+
+    @pl.when(jnp.logical_not(plain))
     def _():
         message_ref[...] = product(h, product(green_ref[...], hd))
 
 
-def inward_kernel(axes, level, _, received, system, green, message, u, v, h, hd, system_ref, green_ref, message_ref, u_ref, v_ref):
+def inward_kernel(axes, level, _, received, system, green, message, u, outside, h, hd, system_ref, green_ref, message_ref, u_ref, outside_ref):
     _, depth, left = place(axes)
 
     @pl.when(depth == level)
@@ -225,17 +220,17 @@
         def _():
             gh = product(got, h[...])
             u_ref[...] = gh
-            v_ref[...] = got
+            outside_ref[...] = got
             system_ref[...] = system[...] - product(hd[...], gh)
 
         @pl.when(jnp.logical_not(left))
         def _():
             system_ref[...] = system[...] - got
             u_ref[...] = u[...]
-            v_ref[...] = v[...]
+            outside_ref[...] = outside[...]
 
         invert(system_ref[...], green_ref)
-        send(left, level == axes[2] // 2 - 1, green_ref, h[...], hd[...], message_ref)
+        send(left, green_ref, h[...], hd[...], message_ref)
 
     @pl.when(depth != level)
     def _():
@@ -243,30 +238,50 @@
         green_ref[...] = green[...]
         message_ref[...] = message[...]
         u_ref[...] = u[...]
-        v_ref[...] = v[...]
-
-
-def middle_kernel(axes, received, system, green, h, hd, following, diagonal_ref, u_ref, token_ref):
+        outside_ref[...] = outside[...]
+
+
+def middle_kernel(axes, received, system, green, h, hd, diagonal_ref, message_ref, u_ref, token_ref):
     token_ref[...] = jnp.zeros_like(token_ref)
     _, depth, left = place(axes)
 
     @pl.when(depth == axes[2] // 2 - 1)
     def _():
         got = received[...]
-        next_h = following[...]
-        right_factor = jnp.where(left, dagger(next_h), h[...])
-        left_factor = jnp.where(left, next_h, hd[...])
-        gh = product(got, right_factor)
-        u_ref[...] = gh
-        invert(system[...] - product(left_factor, gh), diagonal_ref)
+
+        @pl.when(left)
+        def _():
+            u_ref[...] = system[...] - got
+
+        @pl.when(jnp.logical_not(left))
+        def _():
+            message_ref[...] = product(got, h[...])
+            u_ref[...] = system[...] - product(hd[...], message_ref[...])
+
+        s = u_ref[...]
+        u_ref[...] = message_ref[...]
+        invert(s, diagonal_ref)
+        send(jnp.logical_not(left), diagonal_ref, h[...], hd[...], message_ref)
 
     @pl.when(depth != axes[2] // 2 - 1)
     def _():
         diagonal_ref[...] = green[...]
         u_ref[...] = jnp.zeros_like(u_ref)
-
-
-def waiting_kernel(axes, _, received, diagonal, u_in, u_out, outside, h, hd, following, upper_ref, lower_ref, ready_ref):
+        message_ref[...] = jnp.zeros_like(message_ref)
+
+
+def waiting_kernel(axes, extra, *refs):
+    received, diagonal, u_in, u_out, outside, h, hd, *rest = refs[1:]
+    if extra:
+        one, two, upper_ref, lower_ref, ready_ref, first_ref, second_ref, arrivals = rest
+        copies = [
+            pltpu.make_async_copy(one.at[:1], first_ref, arrivals.at[0]),
+            pltpu.make_async_copy(two.at[1:], second_ref, arrivals.at[1]),
+        ]
+        for copy in copies:
+            copy.start()
+    else:
+        upper_ref, lower_ref, ready_ref = rest
     position, depth, left = place(axes)
     energy = energy_point(axes)
     magnitude = energy * energy + BROADEN * BROADEN
@@ -283,34 +298,39 @@
     @pl.when(depth != axes[2] // 2 - 1)
     def _():
         g = diagonal[...]
-        next_h = following[...]
-        right_in = jnp.where(left, dagger(next_h), h[...])
-        left_in = jnp.where(left, next_h, hd[...])
-        p = product(g, left_in)
-        q = product(right_in, g)
-        ready_ref[0] = p
-        ready_ref[1] = q
 
         @pl.when(left)
         def _():
             at_contact = position == 0
             u = jnp.where(at_contact, times_complex(h[...], contact_re, contact_im), u_out[...])
             v = jnp.where(at_contact, times_complex(hd[...], contact_re, contact_im), product(hd[...], outside[...]))
-            ready_ref[2] = product(u, p)
-            ready_ref[3] = product(q, v)
-            ready_ref[4] = product(u, g)
-            ready_ref[5] = product(g, v)
+            ready_ref[0] = g
+            ready_ref[1] = g
+            ready_ref[2] = product(u, g)
+            ready_ref[3] = product(g, v)
+
+        @pl.when(jnp.logical_not(left))
+        def _():
+            ready_ref[0] = product(g, hd[...])
+            ready_ref[1] = product(h[...], g)
+            ready_ref[2] = jnp.zeros_like(g)
+            ready_ref[3] = jnp.zeros_like(g)
 
         upper_ref[...] = jnp.zeros_like(upper_ref)
         lower_ref[...] = jnp.zeros_like(lower_ref)
 
-
-def outward_kernel(axes, level, final, received, ready, diagonal, upper, lower, *outputs):
+    if extra:
+        for copy in copies:
+            copy.wait()
+
+
+def outward_kernel(axes, level, final, received, ready, diagonal, upper, lower, h, hd, *outputs):
     _, depth, left = place(axes)
     if final:
         green_out, packed_ref, green_ref, upper_ref, lower_ref = outputs
     else:
-        green_ref, upper_ref, lower_ref = outputs
+        message_ref, _, green_ref, upper_ref, lower_ref = outputs
+        message_ref[...] = jnp.zeros_like(message_ref)
 
     @pl.when(depth != level)
     def _():
@@ -327,13 +347,16 @@
 
         @pl.when(left)
         def _():
-            upper_ref[...] = ready[4] + product(ready[2], w)
-            lower_ref[...] = ready[5] + product(p, product(g_in, ready[3]))
+            upper_ref[...] = ready[2] + product(ready[2], w)
+            lower_ref[...] = ready[3] + product(p, product(g_in, ready[3]))
 
         @pl.when(jnp.logical_not(left))
         def _():
             upper_ref[...] = w
             lower_ref[...] = product(p, g_in)
+
+        if not final:
+            send(jnp.logical_not(left), green_ref, h[...], hd[...], message_ref)
 
     if final:
         size = diagonal.shape[0]
@@ -363,80 +386,83 @@
     out[2, 1] = pack[2].T
 
 
-def add_term(axes, out, spectral, blocks, index):
-    chips, cores, _ = axes
-    energy = energy_at(index.astype(F32), chips * cores)
-    occupation = 1.0 / (1.0 + jnp.exp(jnp.full((1, 1), energy / THERMAL, F32)))
-    for s, scale in enumerate((-occupation, 1.0 - occupation)):
-        kernel = blocks(s)
-        for b in range(3):
-            w_re, w_im = kernel[b, 0], kernel[b, 1]
-            g_re, g_im = scale * spectral[b, 0], scale * spectral[b, 1]
-            out[s, b, 0] -= g_re * w_im + g_im * w_re
-            out[s, b, 1] += g_re * w_re - g_im * w_im
+def add_term(out, spectral, blocks, scale):
+    for b in range(3):
+        w_re, w_im = blocks[b, 0], blocks[b, 1]
+        g_re, g_im = scale * spectral[b, 0], scale * spectral[b, 1]
+        out[b, 0] -= g_re * w_im + g_im * w_re
+        out[b, 1] += g_re * w_re - g_im * w_im
 
 
 def terms_kernel(axes, same, *refs):
     chips, cores, _ = axes
     packs, rest = refs[:chips], refs[chips:]
-    before, spectral, out = rest[0] if not same else None, rest[-1], rest[-2]
-    pieces = rest[: len(rest) - 2] if same else rest[1 : len(rest) - 2]
-    half = len(pieces) // 2
-    own, other = kernel_blocks(chips, pieces[:half]), kernel_blocks(chips, pieces[half:])
+    before, pieces = ([], rest[:-3]) if same else (rest[:2], rest[2:-3])
+    outs, spectral = rest[-3:-1], rest[-1]
     chip, core = lax.axis_index("chip"), lax.axis_index("core")
-    out[...] = jnp.zeros_like(out) if same else before[...]
+    for i, out in enumerate(outs):
+        out[...] = jnp.zeros_like(out) if same else before[i][...]
     for r in range(chips):
         @pl.when(chip >= r)
         def _():
             unpack(packs[r], spectral.at[r])
     for offset in range(chips):
-        chip_of = jnp.bitwise_xor(chip, offset) if len(pieces) > 2 else jnp.int32(offset)
+        kappa = jnp.bitwise_xor(chip, offset) if len(pieces) > 1 else jnp.int32(offset)
         for c in range(cores):
-            r = chip_of if same else chip_of + 1 - c
-            source = (own if c == 0 else other) if same else (other if c == 0 else own)
-            origin = core if same else 1 - core
-
-            @pl.when(jnp.logical_and(core == c, r <= chip))
-            def _():
-                blocks = functools.partial(source[offset], chip_of)
-                add_term(axes, out, spectral.at[r], blocks, (chip - r) * cores + origin)
+            p = c if same else 1 - c
+            for k in range(cores):
+                r = kappa + (p + k) // 2
+                out = outs[0] if (p + k) % 2 == c else outs[1]
+
+                @pl.when(jnp.logical_and(core == c, r <= chip))
+                def _():
+                    index = (chip - r) * cores + p
+                    energy = energy_at(index.astype(F32), chips * cores)
+                    occupation = 1.0 / (1.0 + jnp.exp(jnp.full((1, 1), energy / THERMAL, F32)))
+                    scale = -occupation if c == 0 else 1.0 - occupation
+                    add_term(out, spectral.at[r], screened_at(pieces, offset, kappa, k), scale)
+
+
+def screened_at(pieces, offset, kappa, k):
+    if len(pieces) == 1:
+        return pieces[0].at[kappa, k]
+    return pieces[offset].at[k] if offset < 3 else pieces[3 + k].at[0]
+
+
+def join_kernel(axes, mine, received, out, arrivals):
+    core = lax.axis_index("core")
+    copies = [
+        pltpu.make_async_copy(mine, out.at[core], arrivals.at[0]),
+        pltpu.make_async_copy(received, out.at[1 - core], arrivals.at[1]),
+    ]
+    for copy in copies:
+        copy.start()
+    for copy in copies:
+        copy.wait()
 
 
 class Exchange:
-    def __init__(self, chips, cores, screened):
+    def __init__(self, chips, screened, swap):
         self.paired = chips == 4
-        self.swap = [(i, i ^ 1) for i in range(cores)] if cores == 2 else []
         self.own = screened[0, 0]
-        self.early = []
-        self.pieces = [self.own] if self.paired else [lax.all_gather(self.own, "chip", axis=0)]
+        core = lax.axis_index("core")
+        self.got = lax.ppermute(jnp.where(core == 0, self.own[1], self.own[0]), "core", swap)
 
     def moved(self, piece, offset):
         return lax.ppermute(piece, "chip", [(i, i ^ offset) for i in range(4)])
 
     def begin(self, after):
+        core = lax.axis_index("core")
+        own, got, _ = lax.optimization_barrier((self.own, self.got, after))
+        pair = jnp.stack([jnp.where(core == 0, own[0], got), jnp.where(core == 0, got, own[1])])
         if self.paired:
-            own, _ = lax.optimization_barrier((self.own, after))
-            self.pieces += [self.moved(own, 1), self.moved(own, 2)]
-
-    def go_on(self, after):
+            self.pieces = [pair, self.moved(pair, 1), self.moved(pair, 2)]
+        else:
+            self.pieces = [lax.all_gather(pair, "chip", axis=0)]
+
+    def go_on(self, halves):
         if self.paired:
-            one, two = self.pieces[1:]
-            one, two, _ = lax.optimization_barrier((one, two, after))
-            self.pieces += [self.moved(one[:1], 2), self.moved(two[1:], 1)]
-            own, one, two, _ = lax.optimization_barrier((*self.pieces[:3], after))
-            self.early = [lax.ppermute(piece, "core", self.swap) for piece in (own, one, two)]
-
-    def finish(self, after):
-        late = self.pieces[3:] if self.paired else self.pieces
-        *late, _ = lax.optimization_barrier((*late, after))
-        return self.pieces, self.early + [lax.ppermute(piece, "core", self.swap) for piece in late]
-
-
-def kernel_blocks(chips, pieces):
-    if len(pieces) == 1:
-        return [(lambda chip_of, kind: pieces[0].at[chip_of, kind])] * chips
-    found = [(lambda chip_of, kind, piece=piece: piece.at[kind]) for piece in pieces[:3]]
-    return found + [lambda chip_of, kind: pieces[3 + kind].at[0]]
+            self.pieces += [self.moved(halves[0], 2), self.moved(halves[1], 1)]
 
 
 def local(axes, onsite, hopping, sigma_old, screened):
@@ -444,13 +470,16 @@
     size = sigma_old.shape[-1]
     half = cells_all // 2
     matrix = jax.ShapeDtypeStruct((size, 2 * size), F32)
-    def call(body, out_shape, *operands, space=pltpu.VMEM, grant=16, work=WORK, **options):
+    def call(body, out_shape, *operands, space=pltpu.VMEM, grant=16, work=WORK, out_space=None, **options):
         spec = pl.BlockSpec(memory_space=pltpu.VMEM)
+        spaces = space if isinstance(space, list) else [space] * len(operands)
         return pl.pallas_call(
             functools.partial(body, axes),
             out_shape=out_shape,
-            in_specs=[pl.BlockSpec(memory_space=space)] * len(operands),
-            out_specs=jax.tree.map(lambda _: spec, out_shape),
+            in_specs=[pl.BlockSpec(memory_space=space) for space in spaces],
+            out_specs=jax.tree.map(lambda _: spec, out_shape)
+            if out_space is None
+            else jax.tree.map(lambda space: pl.BlockSpec(memory_space=space), out_space),
             compiler_params=pltpu.CompilerParams(vmem_limit_bytes=grant * 1024 * 1024),
             cost_estimate=pl.CostEstimate(
                 flops=int(work * 80 * (2 * size) ** 3), bytes_accessed=2 * 1024 * 1024, transcendentals=0
@@ -458,8 +487,8 @@
             **options,
         )(*operands)
 
-    swap = [(i, i ^ 1) for i in range(cores)] if cores == 2 else []
-    exchange = Exchange(chips, cores, screened)
+    swap = [(i, i ^ 1) for i in range(cores)]
+    exchange = Exchange(chips, screened, swap)
     token = jax.ShapeDtypeStruct((8, size), F32)
     system, green, message, h, hd, mark = call(
         outer_kernel,
@@ -471,14 +500,10 @@
     )
     mark = lax.ppermute(mark, "core", swap)
     exchange.begin(mark)
-    h_sent, _ = lax.optimization_barrier((h, mark))
-    following = lax.ppermute(h_sent, "space", [(i + 1, i) for i in range(cells_all - 1)])
     u_out = outside = jnp.zeros((size, 2 * size), F32)
     for level in range(1, half):
         route = [(level - 1, level), (cells_all - level, cells_all - 1 - level)]
         received = lax.ppermute(message, "space", route)
-        if level == 1:
-            received, following = lax.optimization_barrier((received, following))
         system, green, message, u_out, outside = call(
             functools.partial(swapped, inward_kernel, level),
             (matrix,) * 5,
@@ -486,23 +511,29 @@
             work=WORK2,
         )
     received = lax.ppermute(message, "space", [(half - 1, half), (half, half - 1)])
-    diagonal, u_in, mark = call(
-        middle_kernel, (matrix,) * 2 + (token,), received, system, green, h, hd, following,
+    diagonal, message, u_in, mark = call(
+        middle_kernel, (matrix,) * 3 + (token,), received, system, green, h, hd,
         work=WORK3,
     )
     mark = lax.ppermute(mark, "core", swap)
-    exchange.go_on(mark)
+    half_kernels = jax.ShapeDtypeStruct((1, *screened.shape[3:]), F32)
     upper = None
     for level in reversed(range(half - 1)):
         route = [(level + 1, level), (cells_all - 2 - level, cells_all - 1 - level)]
-        arrived = lax.ppermute(diagonal, "space", route)
+        arrived = lax.ppermute(message, "space", route)
         if upper is None:
-            upper, lower, ready = call(
-                waiting_kernel,
-                (matrix, matrix, jax.ShapeDtypeStruct((6, size, 2 * size), F32)),
-                mark, received, diagonal, u_in, u_out, outside, h, hd, following,
+            paired = exchange.paired
+            spaces = [pltpu.VMEM] * 8 + [pl.ANY] * (2 if paired else 0)
+            upper, lower, ready, *halves = call(
+                functools.partial(swapped, waiting_kernel, paired),
+                (matrix, matrix, jax.ShapeDtypeStruct((4, size, 2 * size), F32)) + (half_kernels,) * (2 if paired else 0),
+                mark, received, diagonal, u_in, u_out, outside, h, hd, *(exchange.pieces[1:] if paired else []),
+                space=spaces,
+                out_space=(pltpu.VMEM,) * 3 + (pl.ANY,) * (2 if paired else 0),
+                scratch_shapes=[pltpu.SemaphoreType.DMA((2,))] if paired else [],
                 work=WORK4,
             )
+            exchange.go_on(halves)
         final = level == 0
         shapes = (matrix,) * 3
         if final:
@@ -510,32 +541,38 @@
                 jax.ShapeDtypeStruct((3, 2, size, size), F32),
                 jax.ShapeDtypeStruct((3, size, size), F32),
             ) + shapes
+        else:
+            shapes = (matrix, token) + shapes
         results = call(
             functools.partial(swapped, outward_kernel, level, final),
             shapes,
-            arrived, ready, diagonal, upper, lower,
+            arrived, ready, diagonal, upper, lower, h, hd,
             work=WORK6,
         )
-        diagonal, upper, lower = results[-3:]
+        message, _, diagonal, upper, lower = results
     green_out, packed = results[:2]
     own = [packed] + [
         lax.ppermute(packed, "chip", [(i, i + r) for i in range(chips - r)]) for r in range(1, chips)
     ]
-    if exchange.paired:
-        *arrived, exchange.pieces[3], exchange.pieces[4] = lax.optimization_barrier((*own[1:], *exchange.pieces[3:]))
-        own[1:] = arrived
     other = [lax.ppermute(pack, "core", swap) for pack in own]
-    pieces, other_pieces = exchange.finish(own[1:] if chips > 1 else packed)
-    result = jax.ShapeDtypeStruct((2, 3, 2, size, size), F32)
+    kind = jax.ShapeDtypeStruct(screened.shape[3:], F32)
     unpacked = [pltpu.VMEM((chips, 3, 2, size, size), F32)]
-    partial = call(
-        functools.partial(swapped, terms_kernel, True), result, *own, *pieces, *other_pieces,
+    mine, theirs = call(
+        functools.partial(swapped, terms_kernel, True), (kind,) * 2, *own, *exchange.pieces,
         scratch_shapes=unpacked,
         work=WORK5,
     )
+    mine, theirs = call(
+        functools.partial(swapped, terms_kernel, False), (kind,) * 2, *other, mine, theirs, *exchange.pieces,
+        scratch_shapes=unpacked,
+    )
     sigma_out = call(
-        functools.partial(swapped, terms_kernel, False), result, *other, partial, *pieces, *other_pieces,
-        scratch_shapes=unpacked,
+        join_kernel,
+        jax.ShapeDtypeStruct(screened.shape[2:], F32),
+        mine, lax.ppermute(theirs, "core", swap),
+        space=pl.ANY,
+        out_space=pl.ANY,
+        scratch_shapes=[pltpu.SemaphoreType.DMA((2,))],
     )
     return green_out[None, None], sigma_out[None, None]
 
@@ -547,7 +584,7 @@
 
 
 def solution(mesh):
-    cores = 2 if mesh.shape["energy"] % 2 == 0 else 1
+    cores = 2
     axes = (mesh.shape["energy"] // cores, cores, mesh.shape["space"])
     split_mesh = jax.sharding.Mesh(mesh.devices.reshape(axes), ("chip", "core", "space"))
     energy = ("chip", "core")

time: 63.9 us -> 56 us (0.88)
  waiting for transfers between devices: 34.5 us -> 25 us
  other arithmetic: 0 us -> 1.3 us
    ppermute x7 -> x3, waiting for transfers between devices: 20 us -> 1.42 us  [the longest x1 1.42 us: local(): lax.ppermute(theirs, 'core', swap)]
    ppermute x4, waiting for transfers between devices: 5.83 us -> 16.7 us  [moved(): return lax.ppermute(piece, 'chip', [(i, i ^ offset) for i in range(4)])]
    ppermute x4, starting transfers between devices: 3.6 us -> 5.46 us  [moved(): return lax.ppermute(piece, 'chip', [(i, i ^ offset) for i in range(4)])]
    ppermute x7 -> x3, starting transfers between devices: 3.68 us -> 2.18 us  [the longest x1 1.29 us: local(): arrived = lax.ppermute(message, 'space', route)]
    select_n x0 -> x1, other arithmetic: none -> 1.16 us  [__init__(): jnp.where(core == 0, self.own[1], self.own[0])]
    ppermute x2, waiting for transfers between devices: 1.16 us -> 0.01 us  [local(): mark = lax.ppermute(mark, 'core', swap)]
    pallas_call x7 -> x8, Pallas kernels: 8.28 us -> 8.39 us  [call(): pl.pallas_call(functools.partial(body, axes), out_shape=out_shape, in_spe...]
  transfers between devices with their start and end apart: 22 -> 18, of which waited for: 11 -> 8; matrix products, arithmetic and copies ran while one was open for 0% -> 0% of each run, Pallas kernels for 5% -> 13%
where the time goes in v1:
time: 56 us; the launch traced here: 55.1 us
  waiting for transfers between devices  25 us (45%)
  starting transfers between devices  19.6 us (35%)
  Pallas kernels  8.39 us (15%)
  other arithmetic  1.3 us (2%)
  between operations  0.83 us (1%)
    ppermute x4, waiting for transfers between devices, moved(): return lax.ppermute(piece, 'chip', [(i, i ^ offset) for i in range(4)])  16.7 us
    pallas_call x8, Pallas kernels, call(): pl.pallas_call(functools.partial(body, axes), out_shape=out_shape, in_spe...  8.39 us
    ppermute x3, starting transfers between devices, local(): lax.ppermute(packed, 'chip', [(i, i + r) for i in range(chips - r)])  8.11 us
    ppermute x3, waiting for transfers between devices, local(): lax.ppermute(packed, 'chip', [(i, i + r) for i in range(chips - r)])  5.94 us
    ppermute x4, starting transfers between devices, moved(): return lax.ppermute(piece, 'chip', [(i, i ^ offset) for i in range(4)])  5.46 us
    ppermute x1, starting transfers between devices, local(): received = lax.ppermute(message, 'space', route)  2.29 us
    ppermute x1, waiting for transfers between devices, local(): lax.ppermute(theirs, 'core', swap)  1.42 us
    ppermute x1, starting transfers between devices, local(): arrived = lax.ppermute(message, 'space', route)  1.29 us
  transfers between devices with their start and end apart: 18, of which 8 were waited for; matrix products, arithmetic and copies ran while one was open for 0% of the time, Pallas kernels for 13%

profile of v1, /device:TPU:0, one launch (start us, length us, event | category | flops | bytes accessed | tf_op | source)
XLA Modules:
  0.0 55.1 jit_solution(11896478936870506363)
XLA Ops:
  0.6 1.2 %select_bitcast_fusion = f32[3,2,128,128]{3,2,1,0:T(8,128)S(1)} fusion(f32[1,1,2,3,2,128,128]{6,5,4,3,2,1,0:T(8,128)} %param.7, pred[]{:T(512)S(6)} %eq.2), kind=kLoop, calls=%fused_computation.5 | loop fusion | flops 98304 | bytes 1179649 | tf_op jit(solution)/shard_map/jit(_where)/select_n | solution.py:449
  1.8 0.5 collective-permute-start.5
  2.3 3.8 %shard_map.59 = (f32[128,256]{1,0:T(8,128)S(1)}, f32[128,256]{1,0:T(8,128)S(1)}, f32[128,256]{1,0:T(8,128)S(1)}, f32[128,256]{1,0:T(8,128)S(1)}, f32[128,256]{1,0:T(8,128)S(1)}, /*index=5*/f32[8,128]{1,0:T(8,128)S(1)}) custom-call(f32[1,2,128,128]{3,2,1,0:T(8,128)} %onsite_far.1, f32[1,2,128,128]{3,2,1,0:T(8,128)} %hopping_far.1, ...), custom_call_target="tpu_custom_call" | custom-call | flops 1342177280 | bytes 2097152 | tf_op jit(solution)/shard_map/pallas_call | solution.py:476
  6.3 2.3 %collective-permute-start.1 = (f32[128,256]{1,0:T(8,128)S(1)}, f32[128,256]{1,0:T(8,128)S(1)}, u32[]{:S(2)}, u32[]{:S(2)}) collective-permute-start(f32[128,256]{1,0:T(8,128)S(1)} %get-tuple-element.31.arguments_4_), channel_id=1, source_target_pairs={{0,1},{3,2},{4,5},{7,6},{8,9},{11,10},{12,13},{15,14},{16,17},{19,... | collective-permute-start | bytes 393224 | tf_op jit(solution)/shard_map/ppermute | solution.py:506
  8.8 2.7 %collective-permute-start.7 = (f32[2,3,2,128,128]{4,3,2,1,0:T(8,128)S(1)}, f32[2,3,2,128,128]{4,3,2,1,0:T(8,128)S(1)}, u32[]{:S(2)}, u32[]{:S(2)}) collective-permute-start(f32[2,3,2,128,128]{4,3,2,1,0:T(8,128)S(1)} %pad_maximum_fusion.arguments_4_.arguments_6_), channel_id=1, source_target_pairs={{0,16},{8,24},{16,0},{24,8},{1,17},{9,25},{17,1},{25,9},{2,18},{10... | collective-permute-start | bytes 2359304 | tf_op jit(solution)/shard_map/ppermute | solution.py:452
  11.5 0.8 %collective-permute-start.6 = (f32[2,3,2,128,128]{4,3,2,1,0:T(8,128)S(1)}, f32[2,3,2,128,128]{4,3,2,1,0:T(8,128)S(1)}, u32[]{:S(2)}, u32[]{:S(2)}) collective-permute-start(f32[2,3,2,128,128]{4,3,2,1,0:T(8,128)S(1)} %pad_maximum_fusion.arguments_4_.arguments_6_), channel_id=1, source_target_pairs={{0,8},{8,0},{16,24},{24,16},{1,9},{9,1},{17,25},{25,17},{2,10},{10... | collective-permute-start | bytes 2359304 | tf_op jit(solution)/shard_map/ppermute | solution.py:452
  12.3 0.7 %collective-permute-start.2 = (f32[128,256]{1,0:T(8,128)S(1)}, f32[128,256]{1,0:T(8,128)S(1)}, u32[]{:S(2)}, u32[]{:S(2)}) collective-permute-start(f32[128,256]{1,0:T(8,128)S(1)} %get-tuple-element.36), channel_id=1, source_target_pairs={{1,2},{2,1},{5,6},{6,5},{9,10},{10,9},{13,14},{14,13},{17,18},{18,... | collective-permute-start | bytes 393224 | tf_op jit(solution)/shard_map/ppermute | solution.py:513
  13.1 1.3 %collective-permute-start.3 = (f32[128,256]{1,0:T(8,128)S(1)}, f32[128,256]{1,0:T(8,128)S(1)}, u32[]{:S(2)}, u32[]{:S(2)}) collective-permute-start(f32[128,256]{1,0:T(8,128)S(1)} %get-tuple-element.39), channel_id=1, source_target_pairs={{1,0},{2,3},{5,4},{6,7},{9,8},{10,11},{13,12},{14,15},{17,16},{18,... | collective-permute-start | bytes 393224 | tf_op jit(solution)/shard_map/ppermute | solution.py:523
  14.5 15.2 %collective-permute-done.7.arguments_9_.arguments_6_.arguments_8_ = f32[2,3,2,128,128]{4,3,2,1,0:T(8,128)S(1)} collective-permute-done((f32[2,3,2,128,128]{4,3,2,1,0:T(8,128)S(1)}, f32[2,3,2,128,128]{4,3,2,1,0:T(8,128)S(1)}, u32[]{:S(2)}, u32[]{:S(2)}) %collective-permute-start.7) | collective-permute-done | bytes 786464 | tf_op jit(solution)/shard_map/ppermute | solution.py:452
  29.7 1.5 %collective-permute-done.6.arguments_8_.arguments_5_.arguments_7_ = f32[2,3,2,128,128]{4,3,2,1,0:T(8,128)S(1)} collective-permute-done((f32[2,3,2,128,128]{4,3,2,1,0:T(8,128)S(1)}, f32[2,3,2,128,128]{4,3,2,1,0:T(8,128)S(1)}, u32[]{:S(2)}, u32[]{:S(2)}) %collective-permute-start.6) | collective-permute-done | bytes 786464 | tf_op jit(solution)/shard_map/ppermute | solution.py:452
  31.1 1.0 %shard_map.62 = (f32[128,256]{1,0:T(8,128)S(1)}, f32[128,256]{1,0:T(8,128)S(1)}, f32[4,128,256]{2,1,0:T(8,128)S(1)}, f32[1,3,2,128,128]{4,3,2,1,0:T(8,128)S(1)}, f32[1,3,2,128,128]{4,3,2,1,0:T(8,128)S(1)}) custom-call(f32[8,128]{1,0:T(8,128)S(1)} %collective-permute-done.4.arguments_0_, f32[128,256]{1,0:T(8,128)S(1)} %collective-permute-done.2.received.arguments_1_, ...), custom_call_target="tpu_custom_call" | custom-call | flops 1342177280 | bytes 2097152 | tf_op jit(solution)/shard_map/pallas_call | solution.py:476
  32.1 0.4 collective-permute-start.15
  32.5 1.6 %collective-permute-start.16 = (f32[1,3,2,128,128]{4,3,2,1,0:T(8,128)S(1)}, f32[1,3,2,128,128]{4,3,2,1,0:T(8,128)S(1)}, u32[]{:S(2)}, u32[]{:S(2)}) collective-permute-start(f32[1,3,2,128,128]{4,3,2,1,0:T(8,128)S(1)} %get-tuple-element.53), channel_id=1, source_target_pairs={{0,8},{8,0},{16,24},{24,16},{1,9},{9,1},{17,25},{25,17},{2,10},{10... | collective-permute-start | bytes 1179656 | tf_op jit(solution)/shard_map/ppermute | solution.py:452
  34.1 1.9 %shard_map.63 = (f32[3,2,128,128]{3,2,1,0:T(8,128)}, f32[3,128,128]{2,1,0:T(8,128)S(1)}, f32[128,256]{1,0:T(8,128)}, f32[128,256]{1,0:T(8,128)}, f32[128,256]{1,0:T(8,128)}) custom-call(f32[128,256]{1,0:T(8,128)S(1)} %collective-permute-done.3.arguments_0_, f32[4,128,256]{2,1,0:T(8,128)S(1)} %get-tuple-element.47.arguments_1_, ...), custom_call_target="tpu_custom_call" | custom-call | flops 1342177280 | bytes 2097152 | tf_op jit(solution)/shard_map/pallas_call | solution.py:476
  36.0 4.3 %collective-permute-start.13 = (f32[3,128,128]{2,1,0:T(8,128)S(1)}, f32[3,128,128]{2,1,0:T(8,128)S(1)}, u32[]{:S(2)}, u32[]{:S(2)}) collective-permute-start(f32[3,128,128]{2,1,0:T(8,128)S(1)} %get-tuple-element.51.arguments_0_), channel_id=1, source_target_pairs={{0,24},{1,25},{2,26},{3,27},{4,28},{5,29},{6,30},{7,31}} | collective-permute-start | bytes 589832 | tf_op jit(solution)/shard_map/ppermute | solution.py:555
  40.4 1.3 %collective-permute-start.11 = (f32[3,128,128]{2,1,0:T(8,128)S(1)}, f32[3,128,128]{2,1,0:T(8,128)S(1)}, u32[]{:S(2)}, u32[]{:S(2)}) collective-permute-start(f32[3,128,128]{2,1,0:T(8,128)S(1)} %get-tuple-element.51.arguments_0_), channel_id=1, source_target_pairs={{0,16},{8,24},{1,17},{9,25},{2,18},{10,26},{3,19},{11,27},{4,20},{... | collective-permute-start | bytes 589832 | tf_op jit(solution)/shard_map/ppermute | solution.py:555
  41.7 2.5 %collective-permute-start.9 = (f32[3,128,128]{2,1,0:T(8,128)S(1)}, f32[3,128,128]{2,1,0:T(8,128)S(1)}, u32[]{:S(2)}, u32[]{:S(2)}) collective-permute-start(f32[3,128,128]{2,1,0:T(8,128)S(1)} %get-tuple-element.51.arguments_0_), channel_id=1, source_target_pairs={{0,8},{8,16},{16,24},{1,9},{9,17},{17,25},{2,10},{10,18},{18,26},{... | collective-permute-start | bytes 589832 | tf_op jit(solution)/shard_map/ppermute | solution.py:555
  44.2 2.1 %collective-permute-done.13.arguments_3_ = f32[3,128,128]{2,1,0:T(8,128)S(1)} collective-permute-done((f32[3,128,128]{2,1,0:T(8,128)S(1)}, f32[3,128,128]{2,1,0:T(8,128)S(1)}, u32[]{:S(2)}, u32[]{:S(2)}) %collective-permute-start.13) | collective-permute-done | bytes 196640 | tf_op jit(solution)/shard_map/ppermute | solution.py:555
  46.2 3.9 %collective-permute-done.11.arguments_2_ = f32[3,128,128]{2,1,0:T(8,128)S(1)} collective-permute-done((f32[3,128,128]{2,1,0:T(8,128)S(1)}, f32[3,128,128]{2,1,0:T(8,128)S(1)}, u32[]{:S(2)}, u32[]{:S(2)}) %collective-permute-start.11) | collective-permute-done | bytes 196640 | tf_op jit(solution)/shard_map/ppermute | solution.py:555
  50.1 0.5 collective-permute-start.12
  50.7 0.4 shard_map.64
  51.1 0.5 collective-permute-done.14.arguments_3_
  52.8 1.4 %collective-permute-done.17.received = f32[3,2,128,128]{3,2,1,0:T(8,128)S(1)} collective-permute-done((f32[3,2,128,128]{3,2,1,0:T(8,128)S(1)}, f32[3,2,128,128]{3,2,1,0:T(8,128)S(1)}, u32[]{:S(2)}, u32[]{:S(2)}) %collective-permute-start.17) | collective-permute-done | bytes 393248 | tf_op jit(solution)/shard_map/ppermute | solution.py:572
  54.2 0.9 %shard_map.66 = f32[2,3,2,128,128]{4,3,2,1,0:T(8,128)} custom-call(f32[3,2,128,128]{3,2,1,0:T(8,128)S(1)} %get-tuple-element.56.mine, f32[3,2,128,128]{3,2,1,0:T(8,128)S(1)} %collective-permute-done.17.received), custom_call_target="tpu_custom_call" | custom-call | flops 1342177280 | bytes 2097152 | tf_op jit(solution)/shard_map/pallas_call | solution.py:476
  (26 shorter events, 1.9 us)
Async XLA Ops:
  1.8 6.8 %copy-start = (f32[1,1,2,3,2,128,128]{6,5,4,3,2,1,0:T(8,128)S(1)}, f32[1,1,2,3,2,128,128]{6,5,4,3,2,1,0:T(8,128)}, u32[]{:S(2)}) copy-start(f32[1,1,2,3,2,128,128]{6,5,4,3,2,1,0:T(8,128)} %param.7) | copy-start | bytes 2359300
  1.8 6.8 %collective-permute-start.5 = (f32[3,2,128,128]{3,2,1,0:T(8,128)S(1)}, f32[3,2,128,128]{3,2,1,0:T(8,128)S(1)}, u32[]{:S(2)}, u32[]{:S(2)}) collective-permute-start(f32[3,2,128,128]{3,2,1,0:T(8,128)S(1)} %select_bitcast_fusion), channel_id=1, source_target_pairs={{0,4},{4,0},{1,5},{5,1},{2,6},{6,2},{3,7},{7,3},{8,12},{12,8},{9,1... | collective-permute-start | bytes 1179656 | tf_op jit(solution)/shard_map/ppermute | solution.py:449
  6.1 2.5 %collective-permute-start = (f32[8,128]{1,0:T(8,128)S(1)}, f32[8,128]{1,0:T(8,128)S(1)}, u32[]{:S(2)}, u32[]{:S(2)}) collective-permute-start(f32[8,128]{1,0:T(8,128)S(1)} %get-tuple-element.30), channel_id=1, source_target_pairs={{0,4},{4,0},{1,5},{5,1},{2,6},{6,2},{3,7},{7,3},{8,12},{12,8},{9,1... | collective-permute-start | bytes 12296 | tf_op jit(solution)/shard_map/ppermute | solution.py:501
  6.3 5.9 %collective-permute-start.1 = (f32[128,256]{1,0:T(8,128)S(1)}, f32[128,256]{1,0:T(8,128)S(1)}, u32[]{:S(2)}, u32[]{:S(2)}) collective-permute-start(f32[128,256]{1,0:T(8,128)S(1)} %get-tuple-element.31.arguments_4_), channel_id=1, source_target_pairs={{0,1},{3,2},{4,5},{7,6},{8,9},{11,10},{12,13},{15,14},{16,17},{19,... | collective-permute-start | bytes 393224 | tf_op jit(solution)/shard_map/ppermute | solution.py:506
  8.8 20.9 %collective-permute-start.7 = (f32[2,3,2,128,128]{4,3,2,1,0:T(8,128)S(1)}, f32[2,3,2,128,128]{4,3,2,1,0:T(8,128)S(1)}, u32[]{:S(2)}, u32[]{:S(2)}) collective-permute-start(f32[2,3,2,128,128]{4,3,2,1,0:T(8,128)S(1)} %pad_maximum_fusion.arguments_4_.arguments_6_), channel_id=1, source_target_pairs={{0,16},{8,24},{16,0},{24,8},{1,17},{9,25},{17,1},{25,9},{2,18},{10... | collective-permute-start | bytes 2359304 | tf_op jit(solution)/shard_map/ppermute | solution.py:452
  11.5 19.7 %collective-permute-start.6 = (f32[2,3,2,128,128]{4,3,2,1,0:T(8,128)S(1)}, f32[2,3,2,128,128]{4,3,2,1,0:T(8,128)S(1)}, u32[]{:S(2)}, u32[]{:S(2)}) collective-permute-start(f32[2,3,2,128,128]{4,3,2,1,0:T(8,128)S(1)} %pad_maximum_fusion.arguments_4_.arguments_6_), channel_id=1, source_target_pairs={{0,8},{8,0},{16,24},{24,16},{1,9},{9,1},{17,25},{25,17},{2,10},{10... | collective-permute-start | bytes 2359304 | tf_op jit(solution)/shard_map/ppermute | solution.py:452
  12.3 0.7 %collective-permute-start.2 = (f32[128,256]{1,0:T(8,128)S(1)}, f32[128,256]{1,0:T(8,128)S(1)}, u32[]{:S(2)}, u32[]{:S(2)}) collective-permute-start(f32[128,256]{1,0:T(8,128)S(1)} %get-tuple-element.36), channel_id=1, source_target_pairs={{1,2},{2,1},{5,6},{6,5},{9,10},{10,9},{13,14},{14,13},{17,18},{18,... | collective-permute-start | bytes 393224 | tf_op jit(solution)/shard_map/ppermute | solution.py:513
  13.1 1.4 %collective-permute-start.4 = (f32[8,128]{1,0:T(8,128)S(1)}, f32[8,128]{1,0:T(8,128)S(1)}, u32[]{:S(2)}, u32[]{:S(2)}) collective-permute-start(f32[8,128]{1,0:T(8,128)S(1)} %get-tuple-element.40), channel_id=1, source_target_pairs={{0,4},{4,0},{1,5},{5,1},{2,6},{6,2},{3,7},{7,3},{8,12},{12,8},{9,1... | collective-permute-start | bytes 12296 | tf_op jit(solution)/shard_map/ppermute | solution.py:518
  13.1 21.0 %collective-permute-start.3 = (f32[128,256]{1,0:T(8,128)S(1)}, f32[128,256]{1,0:T(8,128)S(1)}, u32[]{:S(2)}, u32[]{:S(2)}) collective-permute-start(f32[128,256]{1,0:T(8,128)S(1)} %get-tuple-element.39), channel_id=1, source_target_pairs={{1,0},{2,3},{5,4},{6,7},{9,8},{10,11},{13,12},{14,15},{17,16},{18,... | collective-permute-start | bytes 393224 | tf_op jit(solution)/shard_map/ppermute | solution.py:523
  32.1 18.5 %collective-permute-start.15 = (f32[1,3,2,128,128]{4,3,2,1,0:T(8,128)S(1)}, f32[1,3,2,128,128]{4,3,2,1,0:T(8,128)S(1)}, u32[]{:S(2)}, u32[]{:S(2)}) collective-permute-start(f32[1,3,2,128,128]{4,3,2,1,0:T(8,128)S(1)} %get-tuple-element.52), channel_id=1, source_target_pairs={{0,16},{8,24},{16,0},{24,8},{1,17},{9,25},{17,1},{25,9},{2,18},{10... | collective-permute-start | bytes 1179656 | tf_op jit(solution)/shard_map/ppermute | solution.py:452
  32.5 18.2 %collective-permute-start.16 = (f32[1,3,2,128,128]{4,3,2,1,0:T(8,128)S(1)}, f32[1,3,2,128,128]{4,3,2,1,0:T(8,128)S(1)}, u32[]{:S(2)}, u32[]{:S(2)}) collective-permute-start(f32[1,3,2,128,128]{4,3,2,1,0:T(8,128)S(1)} %get-tuple-element.53), channel_id=1, source_target_pairs={{0,8},{8,0},{16,24},{24,16},{1,9},{9,1},{17,25},{25,17},{2,10},{10... | collective-permute-start | bytes 1179656 | tf_op jit(solution)/shard_map/ppermute | solution.py:452
  36.0 10.2 %collective-permute-start.13 = (f32[3,128,128]{2,1,0:T(8,128)S(1)}, f32[3,128,128]{2,1,0:T(8,128)S(1)}, u32[]{:S(2)}, u32[]{:S(2)}) collective-permute-start(f32[3,128,128]{2,1,0:T(8,128)S(1)} %get-tuple-element.51.arguments_0_), channel_id=1, source_target_pairs={{0,24},{1,25},{2,26},{3,27},{4,28},{5,29},{6,30},{7,31}} | collective-permute-start | bytes 589832 | tf_op jit(solution)/shard_map/ppermute | solution.py:555
  40.4 9.7 %collective-permute-start.11 = (f32[3,128,128]{2,1,0:T(8,128)S(1)}, f32[3,128,128]{2,1,0:T(8,128)S(1)}, u32[]{:S(2)}, u32[]{:S(2)}) collective-permute-start(f32[3,128,128]{2,1,0:T(8,128)S(1)} %get-tuple-element.51.arguments_0_), channel_id=1, source_target_pairs={{0,16},{8,24},{1,17},{9,25},{2,18},{10,26},{3,19},{11,27},{4,20},{... | collective-permute-start | bytes 589832 | tf_op jit(solution)/shard_map/ppermute | solution.py:555
  41.7 8.4 %collective-permute-start.9 = (f32[3,128,128]{2,1,0:T(8,128)S(1)}, f32[3,128,128]{2,1,0:T(8,128)S(1)}, u32[]{:S(2)}, u32[]{:S(2)}) collective-permute-start(f32[3,128,128]{2,1,0:T(8,128)S(1)} %get-tuple-element.51.arguments_0_), channel_id=1, source_target_pairs={{0,8},{8,16},{16,24},{1,9},{9,17},{17,25},{2,10},{10,18},{18,26},{... | collective-permute-start | bytes 589832 | tf_op jit(solution)/shard_map/ppermute | solution.py:555
  46.2 4.9 %collective-permute-start.8 = (f32[3,128,128]{2,1,0:T(8,128)S(1)}, f32[3,128,128]{2,1,0:T(8,128)S(1)}, u32[]{:S(2)}, u32[]{:S(2)}) collective-permute-start(f32[3,128,128]{2,1,0:T(8,128)S(1)} %get-tuple-element.51.arguments_0_), channel_id=1, source_target_pairs={{0,4},{4,0},{1,5},{5,1},{2,6},{6,2},{3,7},{7,3},{8,12},{12,8},{9,1... | collective-permute-start | bytes 589832 | tf_op jit(solution)/shard_map/ppermute | solution.py:557
  50.1 1.4 %collective-permute-start.14 = (f32[3,128,128]{2,1,0:T(8,128)S(1)}, f32[3,128,128]{2,1,0:T(8,128)S(1)}, u32[]{:S(2)}, u32[]{:S(2)}) collective-permute-start(f32[3,128,128]{2,1,0:T(8,128)S(1)} %collective-permute-done.13.arguments_3_), channel_id=1, source_target_pairs={{0,4},{4,0},{1,5},{5,1},{2,6},{6,2},{3,7},{7,3},{8,12},{12,8},{9,1... | collective-permute-start | bytes 589832 | tf_op jit(solution)/shard_map/ppermute | solution.py:557
  50.1 1.7 %collective-permute-start.12 = (f32[3,128,128]{2,1,0:T(8,128)S(1)}, f32[3,128,128]{2,1,0:T(8,128)S(1)}, u32[]{:S(2)}, u32[]{:S(2)}) collective-permute-start(f32[3,128,128]{2,1,0:T(8,128)S(1)} %collective-permute-done.11.arguments_2_), channel_id=1, source_target_pairs={{0,4},{4,0},{1,5},{5,1},{2,6},{6,2},{3,7},{7,3},{8,12},{12,8},{9,1... | collective-permute-start | bytes 589832 | tf_op jit(solution)/shard_map/ppermute | solution.py:557
  50.6 1.5 %collective-permute-start.10 = (f32[3,128,128]{2,1,0:T(8,128)S(1)}, f32[3,128,128]{2,1,0:T(8,128)S(1)}, u32[]{:S(2)}, u32[]{:S(2)}) collective-permute-start(f32[3,128,128]{2,1,0:T(8,128)S(1)} %collective-permute-done.9.arguments_1_), channel_id=1, source_target_pairs={{0,4},{4,0},{1,5},{5,1},{2,6},{6,2},{3,7},{7,3},{8,12},{12,8},{9,1... | collective-permute-start | bytes 589832 | tf_op jit(solution)/shard_map/ppermute | solution.py:557
  52.5 1.8 %collective-permute-start.17 = (f32[3,2,128,128]{3,2,1,0:T(8,128)S(1)}, f32[3,2,128,128]{3,2,1,0:T(8,128)S(1)}, u32[]{:S(2)}, u32[]{:S(2)}) collective-permute-start(f32[3,2,128,128]{3,2,1,0:T(8,128)S(1)} %get-tuple-element.57), channel_id=1, source_target_pairs={{0,4},{4,0},{1,5},{5,1},{2,6},{6,2},{3,7},{7,3},{8,12},{12,8},{9,1... | collective-permute-start | bytes 1179656 | tf_op jit(solution)/shard_map/ppermute | solution.py:572
